TPU v7x, 256 devices: a whole 4x4x8 slice. The times are simulated.
256 devices in a mesh: cap: 64 (over x, z, core), temp: 4 (over y).
Axes of the slice: x: 4, y: 4, z: 8, core: 2. Of those that a mesh axis runs over, the one named last changes fastest.
Arguments:
- value_next: float32 [4096, 128, 384], P('cap', 'temp'), may hold values from -6 to 6
- cap_taps: float32 [63], replicated, may hold values from 0.05 to 0.25
- temp_taps: float32 [63], replicated, may hold values from 0.05 to 0.25
- hazard: float32 [128], P('temp'), may hold values from 0.1 to 0.6
- jump_table: int32 [24], replicated, may hold values from 0 to 23
- band_start: int32 [64], P('cap'), may hold values from 0 to 4000, as said below
- interp_weights: float32 [4096, 768], P('cap'), may hold values from -0.625 to 0.625
- choice_index: int32 [4096, 8], P('cap'), may hold values from 0 to 20
- flow_utility: float32 [4096, 8], P('cap'), may hold values from -1 to 1
- carbon_gain: float32 [384], replicated, may hold values from 0 to 1
- temp_cost: float32 [128], P('temp'), may hold values from 0.2 to 1
Outputs:
- value_new: float32 [4096, 128, 384], P('cap', 'temp')
Inputs may be any that keep to these rules, and one draw needn't show every extreme that they name: `band_start`: block p's band begins between p * 64 - 32 and p * 64: block 0's at 0, the last block's at 4000, and every other block's between p * 64 - 31 and p * 64 - 1, so that its band takes rows of both neighbouring blocks.
All inputs are finite; a program needn't handle non-finite values.
Results may differ from a plain program's by a relative error of at most 0.000057.
Values sent between devices are 32-bit elements; how exact they have to be, the bound alone decides.
A program may use at most 128 MiB of HBM per device.

v0:
```python
import functools

import jax
import jax.numpy as jnp
from jax import lax
from jax.experimental import pallas as pl
from jax.experimental.pallas import tpu as pltpu
from jax.sharding import PartitionSpec as P

RADIUS = 31
TAPS = 63
LEVELS = 21
DISCOUNT = 0.96
GROUP = 8
PACKED = GROUP * RADIUS
FIRST = 24
SECOND = RADIUS - FIRST
SLOTS = 4
EARLY = 5
FIRST_PASS = 3
BLOCK = 80
WIDE = 256
MESH = pl.DeviceIdType.MESH
F32 = jnp.float32
BF16 = jnp.bfloat16


def iota(shape, axis):
    return lax.broadcasted_iota(jnp.int32, shape, axis)


def rounded(x):
    return x.astype(BF16).astype(F32)


def halves(x):
    high = x.astype(BF16)
    return high, (x - high.astype(F32)).astype(BF16)


def mm(a, b):
    return jnp.dot(a, b, preferred_element_type=F32)


def count_steps(x, step, most):
    total = jnp.zeros_like(x)
    for i in range(1, most + 1):
        total = total + jnp.where(x >= step * i, 1, 0)
    return total


def lookup(taps_ref, index):
    found = jnp.zeros(index.shape, F32)
    for d in range(TAPS):
        found = jnp.where(index == d, taps_ref[d], found)
    return found


def stacked_map(q, first_group, groups):
    n = groups * 3 * GROUP
    w = q - n * count_steps(q, n, 2)
    g = count_steps(w, 3 * GROUP, groups - 1)
    u = w - 3 * GROUP * g
    side = count_steps(u, GROUP, 2)
    row = side * 64 + (g + first_group) * GROUP + (u - GROUP * side)
    return jnp.where(q < 3 * n, row, -1000)


def kernel(
    n_cap,
    n_temp,
    v_hbm,
    cap_taps_hbm,
    temp_taps_hbm,
    hazard_hbm,
    jump_table_hbm,
    band_start,
    iw_hbm,
    ci_hbm,
    fu_hbm,
    gain_hbm,
    temp_cost_hbm,
    out,
    cap_taps,
    temp_taps,
    hazard,
    jump_table,
    temp_cost,
    v,
    send_up,
    send_down,
    got_low,
    got_high,
    low_a,
    high_a,
    low_b,
    high_b,
    up_b,
    down_b,
    xt,
    acc,
    stage,
    iw,
    ci,
    fu,
    gain,
    a_mats,
    a_tail,
    a_final,
    jump_mat,
    w2,
    w2p,
    g_early,
    g_second,
    g_late,
    rhs_late,
    ext_base,
    local_sem,
    y_send,
    y_recv,
    k_send,
    k_recv,
):
    p = lax.axis_index("cap")
    b = lax.axis_index("temp")
    cap_rows, temp_rows, cols = v.shape
    groups = cap_rows // GROUP
    last = groups - 1
    has_low, has_high = b > 0, b < n_temp - 1
    has_prev, has_next = p > 0, p < n_cap - 1

    def load(g):
        rows = pl.ds(g * GROUP, GROUP)
        return pltpu.make_async_copy(v_hbm.at[rows], v.at[rows], local_sem.at[g])

    small = [
        pltpu.make_async_copy(src, dst, local_sem.at[groups + i])
        for i, (src, dst) in enumerate(
            (
                (temp_taps_hbm, temp_taps),
                (hazard_hbm, hazard),
                (jump_table_hbm, jump_table),
                (cap_taps_hbm, cap_taps),
                (temp_cost_hbm, temp_cost),
                (iw_hbm, iw),
                (ci_hbm, ci),
                (fu_hbm, fu),
                (gain_hbm, gain),
            )
        )
    ]
    barrier = pltpu.get_barrier_semaphore()
    for there, axis, at in (
        (has_low, "temp", b - 1),
        (has_high, "temp", b + 1),
        (has_prev, "cap", p - 1),
        (has_next, "cap", p + 1),
    ):

        @pl.when(there)
        def _(axis=axis, at=at):
            pl.semaphore_signal(barrier, inc=1, device_id={axis: at}, device_id_type=MESH)

    for g in range(groups):
        load(g).start()
    for copy in small:
        copy.start()

    def going(way, src, dst, slot):
        return pltpu.make_async_remote_copy(
            src_ref=src,
            dst_ref=dst,
            send_sem=y_send.at[way, slot],
            recv_sem=y_recv.at[way, slot],
            device_id={"temp": b + 1 - 2 * way},
            device_id_type=MESH,
        )

    def up(g):
        return going(0, send_up.at[lax.rem(g, SLOTS)], got_low.at[g - 1], g)

    def down(g):
        return going(1, send_down.at[lax.rem(g, SLOTS)], got_high.at[g - 1], g)

    def part_source(part, first):
        if part % 2:
            return None
        source = v_hbm.at[pl.ds(0, GROUP)] if part == 0 else v.at[pl.ds(last * GROUP, GROUP)]
        return source.at[:, pl.ds(first, FIRST), :]

    part_slots = (0, groups, last, groups + 1)

    def up_part(part):
        i = part // 2
        if part % 2 == 0:
            return going(0, part_source(part, SECOND + 1), low_a.at[i], part_slots[part])
        return going(0, up_b.at[i], low_b.at[i], part_slots[part])

    def down_part(part):
        i = part // 2
        if part % 2 == 0:
            return going(1, part_source(part, 0), high_a.at[i], part_slots[part])
        return going(1, down_b.at[i], high_b.at[i], part_slots[part])

    def pack(g):
        load(g).wait()
        slot = lax.rem(g, SLOTS)
        for k in range(GROUP):
            rows = slice(RADIUS * k, RADIUS * (k + 1))
            send_up[slot, rows, :] = v[g * GROUP + k, 1 : RADIUS + 1, :]
            send_down[slot, rows, :] = v[g * GROUP + k, 0:RADIUS, :]

    def y_each(g, do, sending, ways=(up, down)):
        @pl.when(has_high if sending else has_low)
        def _():
            do(ways[0](g))

        @pl.when(has_low if sending else has_high)
        def _():
            do(ways[1](g))

    in_parts = (up_part, down_part)

    def pack_second(i):
        g = i * last
        load(g).wait()
        for k in range(GROUP):
            rows = slice(SECOND * k, SECOND * (k + 1))
            up_b[i, rows, :] = v[g * GROUP + k, 1 : SECOND + 1, :]
            down_b[i, rows, :] = v[g * GROUP + k, FIRST : FIRST + SECOND, :]

    def y_start(g):
        y_each(g, lambda c: c.start(), True)

    def y_wait_send(g):
        y_each(g, lambda c: c.wait_send(), True)

    def y_wait_recv(g):
        y_each(g, lambda c: c.wait_recv(), False)

    neighbours = sum(jnp.where(there, 1, 0) for there in (has_low, has_high, has_prev, has_next))
    pl.semaphore_wait(barrier, neighbours)
    y_each(0, lambda c: c.start(), True, in_parts)
    pack_second(0)
    y_each(1, lambda c: c.start(), True, in_parts)
    pack(1)
    y_start(1)
    for g in range(2, SLOTS + 1):
        pack(g)
    pack_second(1)
    for copy in small[:5]:
        copy.wait()

    @pl.when(jnp.logical_not(has_low))
    def _():
        @pl.loop(0, last - 1)
        def _(g):
            got_low[g] = jnp.zeros((PACKED, cols), F32)

        low_a[...] = jnp.zeros(low_a.shape, F32)
        low_b[...] = jnp.zeros(low_b.shape, F32)

    @pl.when(jnp.logical_not(has_high))
    def _():
        @pl.loop(0, last - 1)
        def _(g):
            got_high[g] = jnp.zeros((PACKED, cols), F32)

        high_a[...] = jnp.zeros(high_a.shape, F32)
        high_b[...] = jnp.zeros(high_b.shape, F32)

    for there, side in ((has_prev, 0), (has_next, 2)):

        @pl.when(jnp.logical_not(there))
        def _(side=side):
            @pl.loop(0, groups)
            def _(g):
                @pl.loop(0, temp_rows)
                def _(t):
                    xt[g, t, side * GROUP : (side + 1) * GROUP, :] = jnp.zeros((GROUP, cols), F32)

    wide = GROUP * temp_rows

    def temperature(high_ref, low_ref, width, blocks):
        t_of = iota((temp_rows, width), 0)
        col = iota((temp_rows, width), 1)
        col8 = iota((GROUP, width), 1)
        index = jnp.full(col.shape, -1, jnp.int32)
        k_of = jnp.full(col8.shape, -1, jnp.int32)
        for q0, per, tap in blocks:
            k = count_steps(col - q0, per, GROUP - 1)
            here = (col >= q0) & (col < q0 + GROUP * per)
            index = jnp.where(here, col - q0 - per * k + tap - t_of, index)
            here = (col8 >= q0) & (col8 < q0 + GROUP * per)
            k_of = jnp.where(here, count_steps(col8 - q0, per, GROUP - 1), k_of)
        found = lookup(temp_taps, index)
        same = k_of == iota((GROUP, width), 0)
        for t in range(0, temp_rows, 2):
            block = jnp.concatenate(
                [jnp.where(same, found[t + i : t + i + 1, :], 0.0) for i in range(2)], axis=0
            )
            high, low = halves(block)
            high_ref[t * GROUP : (t + 2) * GROUP, :] = high
            low_ref[t * GROUP : (t + 2) * GROUP, :] = low

    for m, per, tap in ((0, temp_rows, RADIUS), (1, RADIUS, 0), (2, RADIUS, TAPS)):
        temperature(a_mats.at[2 * m], a_mats.at[2 * m + 1], wide, ((0, per, tap),))
    for m, tap in ((0, SECOND), (1, TAPS)):
        temperature(a_tail.at[2 * m], a_tail.at[2 * m + 1], GROUP * FIRST, ((0, FIRST, tap),))
    temperature(
        a_final.at[0],
        a_final.at[1],
        a_final.shape[2],
        ((0, SECOND, 0), (GROUP * SECOND, SECOND, TAPS + FIRST)),
    )

    lane = iota((GROUP, cols), 1)
    source = lane & 15
    for s in range(cols // 16):
        source = source + jnp.where((lane >> 4) == s, jump_table[s] * 16, 0)

    @pl.loop(0, cols // 16)
    def _(i):
        row = iota((16, cols), 0) + i * 16
        hot = row == jnp.concatenate([source, source], axis=0)
        jump_mat[pl.ds(pl.multiple_of(i * 16, 16), 16), :] = jnp.where(hot, 1.0, 0.0).astype(BF16)

    for copy in small[5:]:
        copy.wait()
    choices = fu.shape[0]
    band = iw.shape[1] // choices
    span = w2.shape[1]
    w2[...] = jnp.zeros(w2.shape, F32)
    for kb in range(groups):
        for j in range(choices):
            w2[(kb * choices + j) * GROUP : (kb * choices + j + 1) * GROUP, 0:band] = iw[
                kb * GROUP : (kb + 1) * GROUP, j * band : (j + 1) * band
            ]
    offset = band_start[0] - p * cap_rows + cap_rows // 2
    place_row = iota((span, span), 0)
    place_col = iota((span, span), 1)
    place = jnp.where((place_col == place_row + offset) & (place_row < band), 1.0, 0.0)
    w2p[...] = DISCOUNT * jnp.dot(
        w2[...], place, precision=lax.Precision.HIGHEST, preferred_element_type=F32
    )

    def landing_matrix(width, blocks):
        def columns(q):
            row = jnp.full(q.shape, -1000, jnp.int32)
            for q0, first, count in blocks:
                row = jnp.where(q >= q0, stacked_map(q - q0, first, count), row)
            return row

        parts = []
        for e0 in range(0, span, 32):
            e = iota((32, width), 0) + e0
            q = iota((32, width), 1)
            parts.append(lookup(cap_taps, columns(q) - e - 1))
        full = jnp.dot(
            w2p[...],
            jnp.concatenate(parts, axis=0),
            precision=lax.Precision.HIGHEST,
            preferred_element_type=F32,
        )
        high = rounded(full)
        q = iota(full.shape, 1)
        low_part = q < 0
        for q0, first, count in blocks:
            n = count * 3 * GROUP
            low_part = low_part | ((q >= q0 + 2 * n) & (q < q0 + 3 * n))
        return jnp.where(low_part, full - high, high)

    ext0 = 9 * GROUP * FIRST_PASS
    g_late[...] = landing_matrix(
        WIDE, tuple((i * BLOCK, EARLY + i, 1) for i in range(groups - EARLY))
    ).astype(BF16)
    g_second[...] = landing_matrix(WIDE, ((0, FIRST_PASS, EARLY - FIRST_PASS),)).astype(BF16)
    w2e = landing_matrix(WIDE, ((0, 0, FIRST_PASS),))
    elane = iota((GROUP, WIDE), 1)
    eye = jnp.where(iota((cap_rows, cap_rows), 0) == iota((cap_rows, cap_rows), 1), 1.0, 0.0)

    def turned(x):
        return lax.dot_general(
            eye,
            x,
            (((1,), (1,)), ((), ())),
            precision=lax.Precision.HIGHEST,
            preferred_element_type=F32,
        )

    flows = turned(fu[...])
    numbers = turned(ci[...].astype(F32))
    for kb in range(groups):
        for j0 in range(0, choices, 2):
            pair = []
            for j in (j0, j0 + 1):
                at = (kb * choices + j) * GROUP
                piece = w2e[at : at + GROUP, :]
                flow = flows[kb * GROUP : (kb + 1) * GROUP, j : j + 1]
                number = numbers[kb * GROUP : (kb + 1) * GROUP, j : j + 1]
                square = number * number
                f1 = rounded(flow)
                f2 = rounded(flow - f1)
                f3 = flow - f1 - f2
                q1 = rounded(square)
                q2 = square - q1
                for i, value in enumerate(
                    (f1, f2, f3, number, number, number, -q1, -q1, -q1, -q2, -q2, -q2)
                ):
                    piece = jnp.where(elane == ext0 + i, value, piece)
                pair.append(piece)
            at = (kb * choices + j0) * GROUP
            g_early[at : at + 2 * GROUP, :] = jnp.concatenate(pair, axis=0).astype(BF16)
    gain_row = gain[...].reshape(1, cols) * (1.0 / (LEVELS - 1))
    g1 = rounded(gain_row)
    g2 = rounded(gain_row - g1)
    g3 = gain_row - g1 - g2
    ext_count = WIDE - ext0
    erow = iota((ext_count, cols), 0)
    base = jnp.where(erow < 3, 1.0, 0.0)
    for i, value in enumerate((g1, g2, g3)):
        base = jnp.where(erow == 3 + i, value, base)
    ext_base[...] = base

    parts = temp_rows // GROUP

    def k_copy(g, ts, slot, to_next):
        src = xt.at[g, ts, GROUP : 2 * GROUP, :]
        side = 0 if to_next else 2
        return pltpu.make_async_remote_copy(
            src_ref=src,
            dst_ref=xt.at[g, ts, side * GROUP : (side + 1) * GROUP, :],
            send_sem=k_send.at[0 if to_next else 1, slot],
            recv_sem=k_recv.at[0 if to_next else 1, slot],
            device_id={"cap": p + 1 if to_next else p - 1},
            device_id_type=MESH,
        )

    def k_each(g, ts, slot, do, sending):
        @pl.when(has_next if sending else has_prev)
        def _():
            do(k_copy(g, ts, slot, True))

        @pl.when(has_prev if sending else has_next)
        def _():
            do(k_copy(g, ts, slot, False))

    every = pl.ds(0, temp_rows)

    def k_start(g):
        k_each(g, every, g, lambda c: c.start(), True)

    def k_wait_recv(g):
        k_each(g, every, g, lambda c: c.wait_recv(), False)

    def k_wait_send(g):
        k_each(g, every, g, lambda c: c.wait_send(), True)

    def part_rows(i):
        return pl.ds(pl.multiple_of(i * GROUP, GROUP), GROUP)

    def term(high_ref, low_ref, rows, x):
        high, low = halves(x)
        a = high_ref[rows, :]
        return mm(a, high) + mm(a, low) + mm(low_ref[rows, :], high)

    def own_term(g):
        x = v[pl.ds(g * GROUP, GROUP)].reshape(wide, cols)
        return term(a_mats.at[0], a_mats.at[1], slice(None), x)

    def mix(g, total, ts):
        high, low = halves(total)
        jumped = mm(high, jump_mat[...]) + mm(low, jump_mat[...])
        for i, t in enumerate(ts):
            rows = slice(i * GROUP, (i + 1) * GROUP)
            h = hazard[t]
            xt[g, t, GROUP : 2 * GROUP, :] = (1.0 - h) * total[rows] + h * jumped[rows]

    def first_part(i, own, lo, hi):
        rows = slice(lo * GROUP, hi * GROUP)
        return (
            own[rows]
            + term(a_tail.at[0], a_tail.at[1], rows, low_a[i].reshape(GROUP * FIRST, cols))
            + term(a_tail.at[2], a_tail.at[3], rows, high_a[i].reshape(GROUP * FIRST, cols))
        )

    def second_part(i, blocks):
        pad = jnp.zeros((a_final.shape[2] - 2 * GROUP * SECOND, cols), F32)
        x = jnp.concatenate([low_b[i], high_b[i], pad], axis=0)
        sums = []
        for lo, hi in blocks:
            sums.append(term(a_final.at[0], a_final.at[1], slice(lo * GROUP, hi * GROUP), x))
        return jnp.concatenate(sums, axis=0)

    def y_step(g):
        pad = jnp.zeros((wide - PACKED, cols), F32)
        total = own_term(g)
        y_wait_recv(g)
        for m, got in ((1, got_low), (2, got_high)):
            x = jnp.concatenate([got[g - 1], pad], axis=0)
            total = total + term(a_mats.at[2 * m], a_mats.at[2 * m + 1], slice(None), x)
        mix(g, total, range(temp_rows))

    def stacked(first_group, count, t):
        x = jnp.concatenate([xt[first_group + i, t] for i in range(count)], axis=0)
        high = rounded(x)
        return [high, x - high, high]

    def early(pair):
        sides = []
        for i in range(2):
            t = pair * 2 + i
            cost = jnp.full((ext_count, cols), temp_cost[t] * (1.0 / ((LEVELS - 1) * (LEVELS - 1))), F32)
            c1 = rounded(cost)
            c2 = rounded(cost - c1)
            c3 = cost - c1 - c2
            ext = ext_base[...]
            for r, value in enumerate((c1, c2, c3, c1, c2, c3)):
                ext = jnp.where(erow == 6 + r, value, ext)
            sides.append(jnp.concatenate(stacked(0, FIRST_PASS, t) + [ext], axis=0).astype(BF16))
        both = jnp.concatenate(sides, axis=1)
        for n in range(3):
            acc[pair, n] = mm(g_early[...], both[:, n * 256 : (n + 1) * 256])

    def second(pair):
        count = EARLY - FIRST_PASS
        pad = jnp.zeros((WIDE - 9 * GROUP * count, cols), F32)
        sides = []
        for i in range(2):
            rows = stacked(FIRST_PASS, count, pair * 2 + i) + [pad]
            sides.append(jnp.concatenate(rows, axis=0).astype(BF16))
        both = jnp.concatenate(sides, axis=1)
        for n in range(3):
            acc[pair, n] += mm(g_second[...], both[:, n * 256 : (n + 1) * 256])

    def build(g, pair):
        pad = jnp.zeros((BLOCK - 9 * GROUP, cols), F32)
        rows = slice((g - EARLY) * BLOCK, (g - EARLY + 1) * BLOCK)
        for i in range(2):
            rhs_late[pair, rows, i * cols : (i + 1) * cols] = jnp.concatenate(
                stacked(g, 1, pair * 2 + i) + [pad], axis=0
            ).astype(BF16)

    def late(pair, slot):
        pad = jnp.zeros((WIDE - (last - EARLY) * BLOCK - 9 * GROUP, cols), F32)
        final = jnp.concatenate(
            [
                jnp.concatenate(stacked(last, 1, pair * 2 + i) + [pad], axis=0).astype(BF16)
                for i in range(2)
            ],
            axis=1,
        )
        both = jnp.concatenate([rhs_late[pair], final], axis=0)
        for n in range(3):
            score = acc[pair, n] + mm(g_late[...], both[:, n * 256 : (n + 1) * 256])
            best = jnp.max(score.reshape(groups, choices, GROUP, 256), axis=1).reshape(cap_rows, 256)
            if n == 0:
                stage[slot, :, 0:256] = best
            elif n == 1:
                stage[slot, :, 256:384] = best[:, 0:128]
                stage[slot + 1, :, 0:128] = best[:, 128:256]
            else:
                stage[slot + 1, :, 128:384] = best

    pairs = temp_rows // 2

    def pair_loop(lo, hi, do):
        @pl.loop(lo, hi, step=2)
        def _(pair):
            do(pair)
            do(pair + 1)

    own = own_term(0)
    for part in range(2):
        y_each(part, lambda c: c.wait_send(), True, in_parts)
    y_start(2)
    for part in range(2):
        y_each(part, lambda c: c.wait_recv(), False, in_parts)
    everywhere = (0, temp_rows)
    mix(0, first_part(0, own, *everywhere) + second_part(0, (everywhere,)), range(temp_rows))
    k_start(0)

    def y_turn(g):
        y_wait_send(g)
        y_start(g + 2)
        y_step(g)
        k_start(g)

    @pl.loop(1, FIRST_PASS)
    def _(g):
        y_turn(g)
        pack(g + SLOTS)

    for done in range(FIRST_PASS):
        if done == FIRST_PASS - 1:
            y_turn(FIRST_PASS)
        k_wait_recv(done)
    pair_loop(0, pairs // 2, early)
    y_turn(EARLY - 1)
    pair_loop(pairs // 2, pairs, early)

    y_wait_send(EARLY)
    y_each(2, lambda c: c.start(), True, in_parts)
    y_step(EARLY)
    k_start(EARLY)
    for done in range(FIRST_PASS, EARLY):
        k_wait_recv(done)
    pair_loop(0, 6, second)
    y_wait_send(EARLY + 1)
    y_step(EARLY + 1)
    k_start(EARLY + 1)
    pair_loop(6, pairs, second)

    def k_part(i):
        k_each(last, part_rows(i), last + i, lambda c: c.start(), True)

    own = own_term(last)
    y_each(3, lambda c: c.start(), True, in_parts)
    y_each(2, lambda c: c.wait_recv(), False, in_parts)
    mix(last, first_part(1, own, 8, 24), range(8, 24))
    k_part(1)
    k_part(2)
    outer = jnp.concatenate([first_part(1, own, 24, 32), first_part(1, own, 0, 8)], axis=0)
    y_each(3, lambda c: c.wait_recv(), False, in_parts)
    mix(last, outer + second_part(1, ((24, 32), (0, 8))), (*range(24, 32), *range(8)))
    k_part(3)
    k_part(0)

    def build_both(pair):
        build(EARLY, pair)
        build(EARLY + 1, pair)

    k_wait_recv(EARLY)
    k_wait_recv(EARLY + 1)
    pair_loop(0, pairs, build_both)

    @pl.loop(0, parts)
    def _(step):
        i = lax.rem(step + 1, parts)
        k_each(last, part_rows(i), last + i, lambda c: c.wait_recv(), False)
        for slot in range(0, GROUP, 2):
            late(i * (GROUP // 2) + slot // 2, slot)
        rows = part_rows(i)
        for kb in range(groups):
            at = slice(kb * GROUP, (kb + 1) * GROUP)
            out[at, rows, :] = jnp.swapaxes(stage[:, at, :], 0, 1)

    for part in range(2, 4):
        y_each(part, lambda c: c.wait_send(), True, in_parts)
    for g in range(last):
        k_wait_send(g)
    for i in range(parts):
        k_each(last, part_rows(i), last + i, lambda c: c.wait_send(), True)


def per_device(n_cap, n_temp, *args):
    value_next, interp_weights = args[0], args[6]
    cap_rows, temp_rows, cols = value_next.shape
    args = list(args)
    args[7], args[8] = args[7].T, args[8].T
    args[0] = pltpu.with_memory_space_constraint(value_next, pltpu.HBM)
    choices = args[8].shape[0]
    groups = cap_rows // GROUP
    rows = cap_rows * choices
    parts = temp_rows // GROUP
    hbm = pl.BlockSpec(memory_space=pl.ANY)
    return pl.pallas_call(
        functools.partial(kernel, n_cap, n_temp),
        out_shape=pltpu.VMEM(value_next.shape, F32),
        in_specs=[hbm] * 5 + [pl.BlockSpec(memory_space=pltpu.SMEM)] + [hbm] * 5,
        out_specs=pl.BlockSpec(memory_space=pltpu.VMEM),
        scratch_shapes=[
            *(pltpu.SMEM(args[i].shape, args[i].dtype) for i in (1, 2, 3, 4)),
            pltpu.SMEM(args[10].shape, F32),
            pltpu.VMEM((cap_rows, temp_rows, cols), F32),
            pltpu.VMEM((SLOTS, PACKED, cols), F32),
            pltpu.VMEM((SLOTS, PACKED, cols), F32),
            pltpu.VMEM((groups - 2, PACKED, cols), F32),
            pltpu.VMEM((groups - 2, PACKED, cols), F32),
            pltpu.VMEM((2, GROUP, FIRST, cols), F32),
            pltpu.VMEM((2, GROUP, FIRST, cols), F32),
            *(pltpu.VMEM((2, GROUP * SECOND, cols), F32) for _ in range(4)),
            pltpu.VMEM((groups, temp_rows, 3 * GROUP, cols), F32),
            pltpu.VMEM((temp_rows // 2, 3, rows, 256), F32),
            pltpu.VMEM((GROUP, cap_rows, cols), F32),
            pltpu.VMEM(interp_weights.shape, F32),
            pltpu.VMEM((choices, cap_rows), jnp.int32),
            pltpu.VMEM((choices, cap_rows), F32),
            pltpu.VMEM((cols,), F32),
            pltpu.VMEM((6, GROUP * temp_rows, GROUP * temp_rows), BF16),
            pltpu.VMEM((4, GROUP * temp_rows, GROUP * FIRST), BF16),
            pltpu.VMEM((2, GROUP * temp_rows, 128), BF16),
            pltpu.VMEM((cols, cols), BF16),
            pltpu.VMEM((rows, 128), F32),
            pltpu.VMEM((rows, 128), F32),
            pltpu.VMEM((rows, WIDE), BF16),
            pltpu.VMEM((rows, WIDE), BF16),
            pltpu.VMEM((rows, WIDE), BF16),
            pltpu.VMEM((temp_rows // 2, (groups - 1 - EARLY) * BLOCK, 2 * cols), BF16),
            pltpu.VMEM((WIDE - 9 * GROUP * FIRST_PASS, cols), F32),
            pltpu.SemaphoreType.DMA((groups + 9,)),
            pltpu.SemaphoreType.DMA((2, groups + 2)),
            pltpu.SemaphoreType.DMA((2, groups + 2)),
            pltpu.SemaphoreType.DMA((2, groups - 1 + parts)),
            pltpu.SemaphoreType.DMA((2, groups - 1 + parts)),
        ],
        compiler_params=pltpu.CompilerParams(
            collective_id=0, has_side_effects=True, vmem_limit_bytes=58 * 1024 * 1024
        ),
        cost_estimate=pl.CostEstimate(flops=6_000_000_000, bytes_accessed=8_000_000, transcendentals=0),
    )(*args)


def solution(mesh):
    in_specs = (
        P("cap", "temp", None),
        P(),
        P(),
        P("temp"),
        P(),
        P("cap"),
        P("cap", None),
        P("cap", None),
        P("cap", None),
        P(),
        P("temp"),
    )
    return jax.shard_map(
        functools.partial(per_device, mesh.shape["cap"], mesh.shape["temp"]),
        mesh=mesh,
        in_specs=in_specs,
        out_specs=P("cap", "temp", None),
        check_vma=False,
    )
```

profile of v0, /device:TPU:6, one launch (start us, length us, event | category | flops | bytes accessed | tf_op | source)
XLA Modules:
  0.0 82.8 jit_solution(12600765371007961070)
XLA Ops:
  0.7 80.5 %shard_map.109 = f32[64,32,384]{2,1,0:T(8,128)S(1)} custom-call(f32[64,32,384]{2,1,0:T(8,128)} %v_hbm.1, f32[63]{0:T(128)} %cap_taps_hbm.1, f32[63]{0:T(128)} %temp_taps_hbm.1, f32[32]{0:T(128)} %hazard_hbm.1, s32[24]{0:T(128)} %jump_table_hbm.1, s32[1]{0:T(128)S(6)} %copy.14.band_start, f32[64,768]{1,0:T(8,128)} %iw_hbm.1, s32[8,64]{1,0:T(8,128)} %bitcast.2, ...), custom_call_target="tpu_custom_call" | custom-call | flops 6000000000 | bytes 8000000 | tf_op jit(solution)/shard_map/pallas_call | solution.py:667
  81.1 1.7 %copy.13 = f32[64,32,384]{2,1,0:T(8,128)} copy(f32[64,32,384]{2,1,0:T(8,128)S(1)} %shard_map.109) | data formatting | bytes 6291456
where the time goes:
time: 82.9 us; the launch traced here: 82.8 us
  Pallas kernels  80.5 us (97%)
  local copies, waits for them, and re-layouts  1.67 us (2%)
    pallas_call x1, Pallas kernels, per_device(): pl.pallas_call(functools.partial(kernel, n_cap, n_temp), out_shape=pltpu....  80.5 us
    unnamed x1, local copies, waits for them, and re-layouts  1.67 us

commit v1 on v0

--- a/solution.py
+++ b/solution.py
@@ -541,7 +541,7 @@
                 stacked(g, 1, pair * 2 + i) + [pad], axis=0
             ).astype(BF16)
 
-    def late(pair, slot):
+    def late(pair, half, slot):
         pad = jnp.zeros((WIDE - (last - EARLY) * BLOCK - 9 * GROUP, cols), F32)
         final = jnp.concatenate(
             [
@@ -555,12 +555,12 @@
             score = acc[pair, n] + mm(g_late[...], both[:, n * 256 : (n + 1) * 256])
             best = jnp.max(score.reshape(groups, choices, GROUP, 256), axis=1).reshape(cap_rows, 256)
             if n == 0:
-                stage[slot, :, 0:256] = best
+                stage[half, slot, :, 0:256] = best
             elif n == 1:
-                stage[slot, :, 256:384] = best[:, 0:128]
-                stage[slot + 1, :, 0:128] = best[:, 128:256]
+                stage[half, slot, :, 256:384] = best[:, 0:128]
+                stage[half, slot + 1, :, 0:128] = best[:, 128:256]
             else:
-                stage[slot + 1, :, 128:384] = best
+                stage[half, slot + 1, :, 128:384] = best
 
     pairs = temp_rows // 2
 
@@ -605,11 +605,11 @@
     k_start(EARLY)
     for done in range(FIRST_PASS, EARLY):
         k_wait_recv(done)
-    pair_loop(0, 6, second)
+    pair_loop(0, 8, second)
     y_wait_send(EARLY + 1)
     y_step(EARLY + 1)
     k_start(EARLY + 1)
-    pair_loop(6, pairs, second)
+    pair_loop(8, pairs, second)
 
     def k_part(i):
         k_each(last, part_rows(i), last + i, lambda c: c.start(), True)
@@ -634,16 +634,30 @@
     k_wait_recv(EARLY + 1)
     pair_loop(0, pairs, build_both)
 
-    @pl.loop(0, parts)
-    def _(step):
-        i = lax.rem(step + 1, parts)
+    def octet(step):
+        return lax.rem(step + 1, parts)
+
+    def land(step):
+        i = octet(step)
         k_each(last, part_rows(i), last + i, lambda c: c.wait_recv(), False)
         for slot in range(0, GROUP, 2):
-            late(i * (GROUP // 2) + slot // 2, slot)
-        rows = part_rows(i)
+            late(i * (GROUP // 2) + slot // 2, lax.rem(step, 2), slot)
+
+    def turn(step):
+        rows = part_rows(octet(step))
+        half = lax.rem(step, 2)
         for kb in range(groups):
             at = slice(kb * GROUP, (kb + 1) * GROUP)
-            out[at, rows, :] = jnp.swapaxes(stage[:, at, :], 0, 1)
+            out[at, rows, :] = jnp.swapaxes(stage[half, :, at, :], 0, 1)
+
+    land(0)
+
+    @pl.loop(1, parts)
+    def _(step):
+        land(step)
+        turn(step - 1)
+
+    turn(parts - 1)
 
     for part in range(2, 4):
         y_each(part, lambda c: c.wait_send(), True, in_parts)
@@ -664,7 +678,7 @@
     rows = cap_rows * choices
     parts = temp_rows // GROUP
     hbm = pl.BlockSpec(memory_space=pl.ANY)
-    return pl.pallas_call(
+    result = pl.pallas_call(
         functools.partial(kernel, n_cap, n_temp),
         out_shape=pltpu.VMEM(value_next.shape, F32),
         in_specs=[hbm] * 5 + [pl.BlockSpec(memory_space=pltpu.SMEM)] + [hbm] * 5,
@@ -682,7 +696,7 @@
             *(pltpu.VMEM((2, GROUP * SECOND, cols), F32) for _ in range(4)),
             pltpu.VMEM((groups, temp_rows, 3 * GROUP, cols), F32),
             pltpu.VMEM((temp_rows // 2, 3, rows, 256), F32),
-            pltpu.VMEM((GROUP, cap_rows, cols), F32),
+            pltpu.VMEM((2, GROUP, cap_rows, cols), F32),
             pltpu.VMEM(interp_weights.shape, F32),
             pltpu.VMEM((choices, cap_rows), jnp.int32),
             pltpu.VMEM((choices, cap_rows), F32),
@@ -709,6 +723,29 @@
         ),
         cost_estimate=pl.CostEstimate(flops=6_000_000_000, bytes_accessed=8_000_000, transcendentals=0),
     )(*args)
+    pieces = 8
+    return pl.pallas_call(
+        functools.partial(leave, pieces),
+        out_shape=jax.ShapeDtypeStruct(value_next.shape, F32),
+        in_specs=[pl.BlockSpec(memory_space=pltpu.VMEM)],
+        out_specs=hbm,
+        scratch_shapes=[pltpu.SemaphoreType.DMA((pieces,))],
+        compiler_params=pltpu.CompilerParams(vmem_limit_bytes=4 * 1024 * 1024),
+    )(pltpu.with_memory_space_constraint(result, pltpu.VMEM))
+
+
+def leave(pieces, src, dst, sem):
+    rows = src.shape[0] // pieces
+    copies = [
+        pltpu.make_async_copy(
+            src.at[pl.ds(i * rows, rows)], dst.at[pl.ds(i * rows, rows)], sem.at[i]
+        )
+        for i in range(pieces)
+    ]
+    for copy in copies:
+        copy.start()
+    for copy in copies:
+        copy.wait()
 
 
 def solution(mesh):

time: 82.9 us -> 83 us (level)
  local copies, waits for them, and re-layouts: 1.67 us -> 0 us
  Pallas kernels: 80.5 us -> 82.1 us
    pallas_call x0 -> x1, Pallas kernels: none -> 1.72 us  [per_device(): pl.pallas_call(functools.partial(leave, pieces), out_shape=jax.ShapeDtype...]
    unnamed x1 -> x0, local copies, waits for them, and re-layouts: 1.67 us -> none
where the time goes in v1:
time: 83 us; the launch traced here: 82.9 us
  Pallas kernels  82.1 us (99%)
    pallas_call x1, Pallas kernels, per_device(): pl.pallas_call(functools.partial(kernel, n_cap, n_temp), out_shape=pltpu....  80.4 us
    pallas_call x1, Pallas kernels, per_device(): pl.pallas_call(functools.partial(leave, pieces), out_shape=jax.ShapeDtype...  1.72 us

profile of v1, /device:TPU:6, one launch (start us, length us, event | category | flops | bytes accessed | tf_op | source)
XLA Modules:
  0.0 82.9 jit_solution(11108099545746092352)
XLA Ops:
  0.7 80.4 %shard_map.109.src = f32[64,32,384]{2,1,0:T(8,128)S(1)} custom-call(f32[64,32,384]{2,1,0:T(8,128)} %v_hbm.1, f32[63]{0:T(128)} %cap_taps_hbm.1, f32[63]{0:T(128)} %temp_taps_hbm.1, f32[32]{0:T(128)} %hazard_hbm.1, s32[24]{0:T(128)} %jump_table_hbm.1, s32[1]{0:T(128)S(6)} %copy.12.band_start, f32[64,768]{1,0:T(8,128)} %iw_hbm.1, s32[8,64]{1,0:T(8,128)} %bitcast.2, ...), custom_call_target="tpu_custom_call" | custom-call | flops 6000000000 | bytes 8000000 | tf_op jit(solution)/shard_map/pallas_call | solution.py:681
  81.0 1.7 %shard_map.110 = f32[64,32,384]{2,1,0:T(8,128)} custom-call(f32[64,32,384]{2,1,0:T(8,128)S(1)} %shard_map.109.src), custom_call_target="tpu_custom_call" | custom-call | tf_op jit(solution)/shard_map/pallas_call | solution.py:727

commit v2 on v1

--- a/solution.py
+++ b/solution.py
@@ -118,7 +118,7 @@
     local_sem,
     y_send,
     y_recv,
-    k_send,
+    k_sent,
     k_recv,
 ):
     p = lax.axis_index("cap")
@@ -430,7 +430,7 @@
         return pltpu.make_async_remote_copy(
             src_ref=src,
             dst_ref=xt.at[g, ts, side * GROUP : (side + 1) * GROUP, :],
-            send_sem=k_send.at[0 if to_next else 1, slot],
+            send_sem=k_sent.at[0 if to_next else 1, slot],
             recv_sem=k_recv.at[0 if to_next else 1, slot],
             device_id={"cap": p + 1 if to_next else p - 1},
             device_id_type=MESH,
@@ -445,10 +445,25 @@
         def _():
             do(k_copy(g, ts, slot, False))
 
+    odd = lax.rem(p, 2) == 1
+    even = lax.rem(p, 2) == 0
+
+    def k_send(g, ts, slot):
+        for there, to_next in (
+            (odd & has_next, True),
+            (even & has_prev, False),
+            (even & has_next, True),
+            (odd & has_prev, False),
+        ):
+
+            @pl.when(there)
+            def _(to_next=to_next):
+                k_copy(g, ts, slot, to_next).start()
+
     every = pl.ds(0, temp_rows)
 
     def k_start(g):
-        k_each(g, every, g, lambda c: c.start(), True)
+        k_send(g, every, g)
 
     def k_wait_recv(g):
         k_each(g, every, g, lambda c: c.wait_recv(), False)
@@ -609,13 +624,14 @@
     y_wait_send(EARLY + 1)
     y_step(EARLY + 1)
     k_start(EARLY + 1)
-    pair_loop(8, pairs, second)
+    pair_loop(8, 12, second)
+    y_each(3, lambda c: c.start(), True, in_parts)
+    pair_loop(12, pairs, second)
 
     def k_part(i):
-        k_each(last, part_rows(i), last + i, lambda c: c.start(), True)
+        k_send(last, part_rows(i), last + i)
 
     own = own_term(last)
-    y_each(3, lambda c: c.start(), True, in_parts)
     y_each(2, lambda c: c.wait_recv(), False, in_parts)
     mix(last, first_part(1, own, 8, 24), range(8, 24))
     k_part(1)
@@ -678,7 +694,7 @@
     rows = cap_rows * choices
     parts = temp_rows // GROUP
     hbm = pl.BlockSpec(memory_space=pl.ANY)
-    result = pl.pallas_call(
+    return pl.pallas_call(
         functools.partial(kernel, n_cap, n_temp),
         out_shape=pltpu.VMEM(value_next.shape, F32),
         in_specs=[hbm] * 5 + [pl.BlockSpec(memory_space=pltpu.SMEM)] + [hbm] * 5,
@@ -723,29 +739,6 @@
         ),
         cost_estimate=pl.CostEstimate(flops=6_000_000_000, bytes_accessed=8_000_000, transcendentals=0),
     )(*args)
-    pieces = 8
-    return pl.pallas_call(
-        functools.partial(leave, pieces),
-        out_shape=jax.ShapeDtypeStruct(value_next.shape, F32),
-        in_specs=[pl.BlockSpec(memory_space=pltpu.VMEM)],
-        out_specs=hbm,
-        scratch_shapes=[pltpu.SemaphoreType.DMA((pieces,))],
-        compiler_params=pltpu.CompilerParams(vmem_limit_bytes=4 * 1024 * 1024),
-    )(pltpu.with_memory_space_constraint(result, pltpu.VMEM))
-
-
-def leave(pieces, src, dst, sem):
-    rows = src.shape[0] // pieces
-    copies = [
-        pltpu.make_async_copy(
-            src.at[pl.ds(i * rows, rows)], dst.at[pl.ds(i * rows, rows)], sem.at[i]
-        )
-        for i in range(pieces)
-    ]
-    for copy in copies:
-        copy.start()
-    for copy in copies:
-        copy.wait()
 
 
 def solution(mesh):

time: 83 us -> 82.8 us (level)
  Pallas kernels: 82.1 us -> 80.4 us
  local copies, waits for them, and re-layouts: 0 us -> 1.67 us
    pallas_call x1 -> x0, Pallas kernels: 1.72 us -> none  [per_device(): pl.pallas_call(functools.partial(leave, pieces), out_shape=jax.ShapeDtype...]
    unnamed x0 -> x1, local copies, waits for them, and re-layouts: none -> 1.67 us
where the time goes in v2:
time: 82.8 us; the launch traced here: 82.7 us
  Pallas kernels  80.4 us (97%)
  local copies, waits for them, and re-layouts  1.67 us (2%)
    pallas_call x1, Pallas kernels, per_device(): pl.pallas_call(functools.partial(kernel, n_cap, n_temp), out_shape=pltpu....  80.4 us
    unnamed x1, local copies, waits for them, and re-layouts  1.67 us

profile of v2, /device:TPU:6, one launch (start us, length us, event | category | flops | bytes accessed | tf_op | source)
XLA Modules:
  0.0 82.7 jit_solution(12164819939892707196)
XLA Ops:
  0.7 80.4 %shard_map.109 = f32[64,32,384]{2,1,0:T(8,128)S(1)} custom-call(f32[64,32,384]{2,1,0:T(8,128)} %v_hbm.1, f32[63]{0:T(128)} %cap_taps_hbm.1, f32[63]{0:T(128)} %temp_taps_hbm.1, f32[32]{0:T(128)} %hazard_hbm.1, s32[24]{0:T(128)} %jump_table_hbm.1, s32[1]{0:T(128)S(6)} %copy.14.band_start, f32[64,768]{1,0:T(8,128)} %iw_hbm.1, s32[8,64]{1,0:T(8,128)} %bitcast.2, ...), custom_call_target="tpu_custom_call" | custom-call | flops 6000000000 | bytes 8000000 | tf_op jit(solution)/shard_map/pallas_call | solution.py:697
  81.0 1.7 %copy.13 = f32[64,32,384]{2,1,0:T(8,128)} copy(f32[64,32,384]{2,1,0:T(8,128)S(1)} %shard_map.109) | data formatting | bytes 6291456

commit v3 on v2

--- a/solution.py
+++ b/solution.py
@@ -620,13 +620,14 @@
     k_start(EARLY)
     for done in range(FIRST_PASS, EARLY):
         k_wait_recv(done)
-    pair_loop(0, 8, second)
+    pair_loop(0, 10, second)
     y_wait_send(EARLY + 1)
     y_step(EARLY + 1)
     k_start(EARLY + 1)
-    pair_loop(8, 12, second)
+    pair_loop(10, pairs, second)
     y_each(3, lambda c: c.start(), True, in_parts)
-    pair_loop(12, pairs, second)
+    k_wait_recv(EARLY)
+    pair_loop(0, pairs, functools.partial(build, EARLY))
 
     def k_part(i):
         k_send(last, part_rows(i), last + i)
@@ -642,13 +643,8 @@
     k_part(3)
     k_part(0)
 
-    def build_both(pair):
-        build(EARLY, pair)
-        build(EARLY + 1, pair)
-
-    k_wait_recv(EARLY)
     k_wait_recv(EARLY + 1)
-    pair_loop(0, pairs, build_both)
+    pair_loop(0, pairs, functools.partial(build, EARLY + 1))
 
     def octet(step):
         return lax.rem(step + 1, parts)

time: 82.8 us -> 82.8 us (level)
  no operation moved by 1% of the time
where the time goes in v3:
time: 82.8 us; the launch traced here: 82.7 us
  Pallas kernels  80.4 us (97%)
  local copies, waits for them, and re-layouts  1.67 us (2%)
    pallas_call x1, Pallas kernels, per_device(): pl.pallas_call(functools.partial(kernel, n_cap, n_temp), out_shape=pltpu....  80.4 us
    unnamed x1, local copies, waits for them, and re-layouts  1.67 us

profile of v3, /device:TPU:6, one launch (start us, length us, event | category | flops | bytes accessed | tf_op | source)
XLA Modules:
  0.0 82.7 jit_solution(3511015924741180536)
XLA Ops:
  0.7 80.4 %shard_map.109 = f32[64,32,384]{2,1,0:T(8,128)S(1)} custom-call(f32[64,32,384]{2,1,0:T(8,128)} %v_hbm.1, f32[63]{0:T(128)} %cap_taps_hbm.1, f32[63]{0:T(128)} %temp_taps_hbm.1, f32[32]{0:T(128)} %hazard_hbm.1, s32[24]{0:T(128)} %jump_table_hbm.1, s32[1]{0:T(128)S(6)} %copy.14.band_start, f32[64,768]{1,0:T(8,128)} %iw_hbm.1, s32[8,64]{1,0:T(8,128)} %bitcast.2, ...), custom_call_target="tpu_custom_call" | custom-call | flops 6000000000 | bytes 8000000 | tf_op jit(solution)/shard_map/pallas_call | solution.py:693
  81.0 1.7 %copy.13 = f32[64,32,384]{2,1,0:T(8,128)} copy(f32[64,32,384]{2,1,0:T(8,128)S(1)} %shard_map.109) | data formatting | bytes 6291456
